TPU v7x, 256 devices: a whole 4x4x8 slice. The times are simulated.
256 devices in a mesh: replica: 16 (over x, z_hi, core), shard: 16 (over z_lo, y).
Axes of the slice: x: 4, y: 4, z: 8 (z_hi: 2, z_lo: 4; z = z_hi * 4 + z_lo), core: 2. Of those that a mesh axis runs over, the one named last changes fastest.
Arguments:
- tokens: bfloat16 [131072, 4096], P(('replica', 'shard')), may hold values from -6 to 6
- cotangent: bfloat16 [131072, 1792], P(('replica', 'shard')), may hold values from -6 to 6
- pseudo_grad: bfloat16 [16, 4096, 1792], P('replica', 'shard'), may hold values from -6 to 6
- anchor: float32 [4096, 1792], P(('shard', 'replica')), may hold values from -6 to 6
- momentum: float32 [4096, 1792], P(('shard', 'replica')), may hold values from -6 to 6
Outputs:
- new_anchor: float32 [4096, 1792], P(('shard', 'replica'))
- new_momentum: float32 [4096, 1792], P(('shard', 'replica'))
- up_acts: bfloat16 [131072, 1792], P(('replica', 'shard'))
- weight_grad: bfloat16 [16, 4096, 1792], P('replica', 'shard')
All inputs are finite; a program needn't handle non-finite values.
Results may differ from a plain program's by a relative error of at most 0.0049.
Values may be sent and summed in bfloat16 or wider, within the bound.
No kernel may reach another device: no remote copies, remote signals or barrier semaphores. Data moves between devices by JAX's collectives and lax.ppermute only.
A program may use at most 128 MiB of HBM per device.

v0:
```python
import jax
import jax.numpy as jnp
from jax import lax
from jax.sharding import PartitionSpec as P

outer_rate = 0.7
momentum_decay = 0.9


def on_device(tokens, cotangent, pseudo_grad, anchor, momentum):
    factor = tokens.shape[1] ** (-0.5)
    replicas = lax.axis_size("replica")
    summed = lax.psum_scatter(
        pseudo_grad[0].astype(jnp.float32), "replica", scatter_dimension=0, tiled=True
    )
    mean_delta = summed / replicas
    moment_out = momentum_decay * momentum + mean_delta
    anchor_out = anchor - outer_rate * (mean_delta + momentum_decay * moment_out)
    group_rows = lax.all_gather(anchor_out.astype(jnp.bfloat16), "replica", axis=0, tiled=True)
    columns = tokens
    acts = jnp.dot(
        columns,
        lax.all_gather(group_rows, "shard", axis=0, tiled=True),
        preferred_element_type=jnp.float32,
    )
    up_acts = (acts * factor).astype(jnp.bfloat16)
    columns = tokens
    summed = lax.psum_scatter(
        lax.dot_general(
            columns, cotangent, (((0,), (0,)), ((), ())), preferred_element_type=jnp.float32
        )
        * factor,
        "shard",
        scatter_dimension=0,
        tiled=True,
    )
    weight_grad = summed.astype(jnp.bfloat16)[None]
    return (anchor_out, moment_out, up_acts, weight_grad)


def solution(mesh):
    in_specs = (
        P(("replica", "shard"), None),
        P(("replica", "shard"), None),
        P("replica", "shard", None),
        P(("shard", "replica"), None),
        P(("shard", "replica"), None),
    )
    out_specs = (
        P(("shard", "replica"), None),
        P(("shard", "replica"), None),
        P(("replica", "shard"), None),
        P("replica", "shard", None),
    )
    return jax.shard_map(
        on_device, mesh=mesh, in_specs=in_specs, out_specs=out_specs, check_vma=False
    )
```

profile of v0, /device:TPU:1, one launch (start us, length us, event | category | flops | bytes accessed | tf_op | source)
XLA Modules:
  0.0 623.4 jit_solution(14021185365393531953)
XLA Ops:
  7.2 0.0 copy-start
  7.2 0.0 copy-start.2
  7.2 0.0 copy-start.1
  7.2 0.0 reduce-scatter.3.cloned.1.call-start
  7.2 2.7 bitcast_convert_fusion
  9.9 0.0 reduce-scatter.3.cloned.1.call-update
  9.9 0.0 all-gather.2.cloned.1.call-start
  10.0 90.6 %reduce-scatter.3.cloned.1.call-done = f32[16,1792]{1,0:T(8,128)} async-done(((f32[256,1792]{1,0:T(8,128)}), f32[16,1792]{1,0:T(8,128)}) %reduce-scatter.3.cloned.1.call-update) | async-done | bytes 114704 | tf_op jit(solution)/shard_map/reduce_scatter | solution.py:13
  100.6 0.0 copy-done.2
  100.6 0.0 copy-done.1
  100.6 1.6 fusion.1
  102.2 36.2 %all_gather.6 = bf16[256,1792]{1,0:T(8,128)(2,1)} all-gather(bf16[16,1792]{1,0:T(8,128)(2,1)S(1)} %get-tuple-element.8), channel_id=1, replica_groups=mesh['replica'=16,'shard'=16] {'replica'}, dimensions={0}, use_global_device_ids=true | all-gather | bytes 974848 | tf_op jit(solution)/shard_map/all_gather | solution.py:19
  138.4 0.0 all-gather.2.cloned.1.call-update
  138.4 0.0 reduce-scatter.5.cloned.1.call-start
  138.4 0.0 copy-done
  138.5 16.6 %convolution_multiply_fusion = f32[4096,1792]{1,0:T(8,128)} fusion(bf16[512,4096]{1,0:T(8,128)(2,1)} %param.5, bf16[512,1792]{1,0:T(8,128)(2,1)S(1)} %copy-done), kind=kOutput, calls=%fused_computation | convolution fusion | flops 7523532800 | bytes 35389440 | tf_op jit(solution)/shard_map/dot_general | solution.py:29
  155.1 0.0 reduce-scatter.5.cloned.1.call-update
  155.1 145.7 %all-gather.2.cloned.1.call-done = bf16[4096,1792]{1,0:T(8,128)(2,1)} async-done(((bf16[256,1792]{1,0:T(8,128)(2,1)}), bf16[4096,1792]{1,0:T(8,128)(2,1)}) %all-gather.2.cloned.1.call-update) | async-done | bytes 14680080 | tf_op jit(solution)/shard_map/all_gather | solution.py:23
  300.8 13.3 %fusion = bf16[512,1792]{0,1:T(8,128)(2,1)} fusion(bf16[4096,1792]{1,0:T(8,128)(2,1)} %all-gather.2.cloned.1.call-done, bf16[512,4096]{1,0:T(8,128)(2,1)} %param.5), kind=kOutput, calls=%fused_computation.2 | convolution fusion | flops 7518027776 | bytes 20709376 | tf_op jit(solution)/shard_map/dot_general | solution.py:21
  314.1 3.8 copy.9
  317.8 296.5 %reduce-scatter.5.cloned.1.call-done = f32[256,1792]{1,0:T(8,128)} async-done(((f32[4096,1792]{1,0:T(8,128)}), f32[256,1792]{1,0:T(8,128)}) %reduce-scatter.5.cloned.1.call-update) | async-done | bytes 1835024 | tf_op jit(solution)/shard_map/reduce_scatter | solution.py:28
  614.3 2.5 convert_bitcast_fusion
Async XLA Ops:
  7.2 131.3 %copy-start = (bf16[512,1792]{1,0:T(8,128)(2,1)S(1)}, bf16[512,1792]{1,0:T(8,128)(2,1)}, u32[]{:S(2)}) copy-start(bf16[512,1792]{1,0:T(8,128)(2,1)} %param.6) | copy-start | bytes 5505028
  7.2 93.4 %copy-start.2 = (f32[16,1792]{1,0:T(8,128)S(1)}, f32[16,1792]{1,0:T(8,128)}, u32[]{:S(2)}) copy-start(f32[16,1792]{1,0:T(8,128)} %param.9) | copy-start | bytes 344068
  7.2 93.4 %copy-start.1 = (f32[16,1792]{1,0:T(8,128)S(1)}, f32[16,1792]{1,0:T(8,128)}, u32[]{:S(2)}) copy-start(f32[16,1792]{1,0:T(8,128)} %param.8) | copy-start | bytes 344068
  7.2 93.4 %reduce-scatter.3.cloned.1.call-start = ((), (), s32[]{:S(2)}) async-start(), calls=%async_computation.2 | async-start | bytes 1949696 | tf_op jit(solution)/shard_map/reduce_scatter | solution.py:13
  9.9 290.8 %all-gather.2.cloned.1.call-start = ((), (), s32[]{:S(2)}) async-start(), calls=%async_computation.3 | async-start | bytes 15597568 | tf_op jit(solution)/shard_map/all_gather | solution.py:23
  138.4 475.9 %reduce-scatter.5.cloned.1.call-start = ((), (), s32[]{:S(2)}) async-start(), calls=%async_computation.4 | async-start | bytes 31195136 | tf_op jit(solution)/shard_map/reduce_scatter | solution.py:28
Sparse Core Ops, SparseCore 0:
  12.8 87.7 reduce-scatter.2
  138.5 162.2 all-gather.1
  303.5 310.7 reduce-scatter.4
where the time goes:
time: 624 us; the launch traced here: 623 us
  waiting for transfers between devices  533 us (85%)
  blocking collectives  36.2 us (6%)
  matrix products  29.9 us (5%)
  between operations  13.8 us (2%)
  other arithmetic  6.79 us (1%)
    reduce_scatter x1, waiting for transfers between devices, on_device(): lax.psum_scatter(lax.dot_general(columns, cotangent, (((0,), (0,)), ((),...  297 us
    all_gather x1, waiting for transfers between devices, on_device(): lax.all_gather(group_rows, 'shard', axis=0, tiled=True)  146 us
    reduce_scatter x1, waiting for transfers between devices, on_device(): lax.psum_scatter(pseudo_grad[0].astype(jnp.float32), 'replica', scatter_d...  90.6 us
    all_gather x1, blocking collectives, on_device(): lax.all_gather(anchor_out.astype(jnp.bfloat16), 'replica', axis=0, tiled=...  36.2 us
    dot_general x1, matrix products, on_device(): lax.dot_general(columns, cotangent, (((0,), (0,)), ((), ())), preferred_e...  16.6 us
    dot_general x1, matrix products, on_device(): jnp.dot(columns, lax.all_gather(group_rows, 'shard', axis=0, tiled=True),...  13.3 us
  transfers between devices with their start and end apart: 3, of which 3 were waited for; matrix products, arithmetic and copies ran while one was open for 5% of the time, Pallas kernels for 0%

commit v1 on v0

v1 whole, which is shorter than its diff:
```python
import functools

import jax
import jax.numpy as jnp
from jax import lax
from jax.experimental import pallas as pl
from jax.experimental.pallas import tpu as pltpu
from jax.sharding import PartitionSpec as P

outer_rate = 0.7
momentum_decay = 0.9

AXES = ("replica", "shard")
f32 = jnp.float32
bf16 = jnp.bfloat16
HALF = 896
VMEM = 56 * 2**20


def place(x, zh, c, zl, y):
    return (((x % 4) * 2 + zh) * 2 + c) * 16 + zl * 4 + y % 4


def table(move):
    pairs = []
    for x in range(4):
        for zh in range(2):
            for c in range(2):
                for zl in range(4):
                    for y in range(4):
                        pairs.append((place(x, zh, c, zl, y), place(*move(x, zh, c, zl, y))))
    return pairs


def x_by(d):
    return table(lambda x, zh, c, zl, y: (x + d, zh, c, zl, y))


def y_by(d):
    return table(lambda x, zh, c, zl, y: (x, zh, c, zl, y + d))


def zl_by(d):
    return table(lambda x, zh, c, zl, y: (x, zh, c, (zl + d) % 4, y))


CORE = table(lambda x, zh, c, zl, y: (x, zh, 1 - c, zl, y))
ZH = table(lambda x, zh, c, zl, y: (x, 1 - zh, c, zl, y))
ZL1 = table(lambda x, zh, c, zl, y: (x, zh, c, zl ^ 1, y))
ZL2 = table(lambda x, zh, c, zl, y: (x, zh, c, zl ^ 2, y))
X_AHEAD = table(lambda x, zh, c, zl, y: (x + 1 - 2 * c, zh, c, zl, y))
X_BACK = table(lambda x, zh, c, zl, y: (x - 1 + 2 * c, zh, c, zl, y))
Y_AHEAD = table(lambda x, zh, c, zl, y: (x, zh, c, zl, y + 1 - 2 * c))
Y_BACK = table(lambda x, zh, c, zl, y: (x, zh, c, zl, y - 1 + 2 * c))


def send(array, pairs):
    return lax.ppermute(array, AXES, pairs)


def gate_body(*refs):
    pass


def gate(array, *first):
    return pl.pallas_call(
        gate_body,
        in_specs=[pl.BlockSpec(memory_space=pl.ANY)] * (1 + len(first)),
        out_specs=pl.BlockSpec(memory_space=pl.ANY),
        out_shape=jax.ShapeDtypeStruct(array.shape, array.dtype),
        input_output_aliases={0: 0},
        compiler_params=pltpu.CompilerParams(vmem_limit_bytes=VMEM),
        cost_estimate=pl.CostEstimate(flops=0, bytes_accessed=0, transcendentals=0),
    )(array, *first)


def pick(array, at, axis=0):
    return lax.dynamic_index_in_dim(array, at, axis, keepdims=False)


def half_of(array, at):
    return jnp.where(at == 0, array[..., :HALF], array[..., HALF:])


def by_index(at, low, high):
    return jnp.stack([jnp.where(at == 0, low, high), jnp.where(at == 0, high, low)])


def stack_body(count, at, *refs):
    out = refs[-1]
    for k, ref in enumerate(refs[:count]):
        out[:, at[k]] = ref[...]


def ring_stack(parts, at, *after):
    first, *rest = parts[0].shape
    shape = (first, len(parts), *rest)
    return pl.pallas_call(
        functools.partial(stack_body, len(parts)),
        in_specs=[pl.BlockSpec(memory_space=pltpu.SMEM)]
        + [pl.BlockSpec(memory_space=pltpu.VMEM)] * len(parts)
        + [pl.BlockSpec(memory_space=pl.ANY)] * len(after),
        out_specs=pl.BlockSpec(memory_space=pltpu.VMEM),
        out_shape=jax.ShapeDtypeStruct(shape, parts[0].dtype),
        compiler_params=pltpu.CompilerParams(vmem_limit_bytes=VMEM),
        cost_estimate=pl.CostEstimate(flops=0, bytes_accessed=0, transcendentals=0),
    )(jnp.stack(at).astype(jnp.int32) % 4, *parts, *after)


def pack_body(width, count, at, *refs):
    out = refs[-1]
    first = width[1] if width else 0
    if width:
        out[:, :first] = refs[0][...]
    for k in range(count):
        out[:, first + 256 * k : first + 256 * (k + 1)] = refs[1 + k][...]


def pack(cot, tokens, width, at, *after):
    count = at.shape[0]
    rows = tokens.shape[0]
    half = width[0] // HALF if width else 0
    columns = 256 * count + (width[1] if width else 0)
    step = rows // 2

    def block(k):
        return pl.BlockSpec((step, 256), lambda i, at: (i, at[k]))

    return pl.pallas_call(
        functools.partial(pack_body, width, count),
        grid_spec=pltpu.PrefetchScalarGridSpec(
            num_scalar_prefetch=1,
            grid=(2,),
            in_specs=[pl.BlockSpec((step, HALF if width else 128), lambda i, at: (i, half))]
            + [block(k) for k in range(count)]
            + [pl.BlockSpec(memory_space=pl.ANY)] * len(after),
            out_specs=pl.BlockSpec((step, columns), lambda i, at: (i, 0)),
        ),
        out_shape=jax.ShapeDtypeStruct((rows, columns), tokens.dtype),
        compiler_params=pltpu.CompilerParams(vmem_limit_bytes=VMEM),
        cost_estimate=pl.CostEstimate(flops=0, bytes_accessed=0, transcendentals=0),
    )(jnp.zeros((1,), jnp.int32) if count == 0 else at.astype(jnp.int32), cot, *[tokens] * count, *after)


def term_body(factor, spec, at, *refs):
    count, fars, cots = spec
    nears, refs = refs[:count], refs[count:]
    far_refs, refs = refs[:fars], refs[fars:]
    cot, far_cots, outs = refs[0], refs[1 : 1 + len(cots)], refs[-count:]
    contract = (((0,), (0,)), ((), ()))

    def add(half):
        low = cots[half]
        near = jnp.concatenate([ref[...] for ref in nears], axis=1)
        far = [ref[...] if ref.shape[1] != HALF + 512 else ref[:, HALF:] for ref in far_refs]
        far = jnp.concatenate(far, axis=1)
        far_cot = far_cots[half][:, low : low + HALF]
        total = lax.dot_general(near, cot[...], contract, preferred_element_type=f32)
        total = total + lax.dot_general(far, far_cot, contract, preferred_element_type=f32)
        for k, out in enumerate(outs):
            out[...] = (total[256 * k : 256 * (k + 1)] * factor).astype(out.dtype)

    for half in range(len(cots)):
        pl.when(pl.program_id(0) == half)(functools.partial(add, half))


def terms(at, tokens, fars, cotangent, half, far_cots, factor, kinds, *after):
    tok = tokens.shape[0]
    count, halves = len(kinds), len(far_cots)

    def near(k):
        return pl.BlockSpec((tok, 256), lambda h, at: (0, at[k]))

    def far(first, columns):
        return pl.BlockSpec((tok, columns), lambda h, at: (0, first // columns))

    return pl.pallas_call(
        functools.partial(term_body, factor, (count, len(fars), tuple(low for _, low in far_cots))),
        grid_spec=pltpu.PrefetchScalarGridSpec(
            num_scalar_prefetch=1,
            grid=(halves,),
            in_specs=[near(k) for k in range(count)]
            + [far(first, columns) for _, first, columns in fars]
            + [pl.BlockSpec((tok, HALF), lambda h, at: (0, half + h))]
            + [pl.BlockSpec(array.shape, lambda h, at: (0, 0)) for array, _ in far_cots]
            + [pl.BlockSpec(memory_space=pl.ANY)] * len(after),
            out_specs=[pl.BlockSpec((256, HALF), lambda h, at: (0, h))] * count,
        ),
        out_shape=[jax.ShapeDtypeStruct((256, HALF * halves), kind) for kind in kinds],
        compiler_params=pltpu.CompilerParams(vmem_limit_bytes=VMEM),
        cost_estimate=pl.CostEstimate(flops=0, bytes_accessed=0, transcendentals=0),
    )(
        at.astype(jnp.int32),
        *[tokens] * count,
        *[array for array, _, _ in fars],
        cotangent,
        *[array for array, _ in far_cots],
        *after,
    )


def act_body(factor, at, mine, other, *refs):
    pieces, (out_mine, out_other, block, sum_mine, sum_other) = refs[:4], refs[-5:]
    step = pl.program_id(0)
    shards = block.shape[0]
    for k, piece in enumerate(pieces):
        block[:, at[k]] = piece[...].reshape(shards, 64, HALF)
    held = block[...].reshape(shards * 256, HALF)
    for tokens, total, out in ((mine, sum_mine, out_mine), (other, sum_other, out_other)):
        part = jnp.dot(tokens[...], held, preferred_element_type=f32)

        @pl.when(step == 0)
        def _(total=total, part=part):
            total[...] = part

        @pl.when(step > 0)
        def _(total=total, part=part):
            total[...] += part

        @pl.when(step == pl.num_programs(0) - 1)
        def _(total=total, out=out):
            out[...] = (total[...] * factor).astype(out.dtype)


def activations(mine, other, pieces, at, factor, *after):
    tok, depth = mine.shape
    shards = 4
    rows = pl.BlockSpec((tok, shards * 256), lambda i, at: (0, i))
    piece = pl.BlockSpec((shards * 64, HALF), lambda i, at: (i, 0))
    whole = pl.BlockSpec((tok, HALF), lambda i, at: (0, 0))
    return pl.pallas_call(
        functools.partial(act_body, factor),
        grid_spec=pltpu.PrefetchScalarGridSpec(
            num_scalar_prefetch=1,
            grid=(depth // (shards * 256),),
            in_specs=[rows, rows] + [piece] * 4 + [pl.BlockSpec(memory_space=pl.ANY)] * len(after),
            out_specs=[whole, whole],
            scratch_shapes=[
                pltpu.VMEM((shards, 4, 64, HALF), bf16),
                pltpu.VMEM((tok, HALF), f32),
                pltpu.VMEM((tok, HALF), f32),
            ],
        ),
        out_shape=[jax.ShapeDtypeStruct((tok, HALF), bf16)] * 2,
        compiler_params=pltpu.CompilerParams(vmem_limit_bytes=VMEM),
        cost_estimate=pl.CostEstimate(flops=0, bytes_accessed=0, transcendentals=0),
    )(jnp.stack(at).astype(jnp.int32) % 4, mine, other, *pieces, *after)


def on_device(tokens, cotangent, pseudo_grad, anchor, momentum):
    factor = tokens.shape[1] ** (-0.5)
    replicas = lax.axis_size("replica")
    replica, shard = lax.axis_index("replica"), lax.axis_index("shard")
    x, zh, c = replica // 4, (replica // 2) % 2, replica % 2
    zl, y = shard // 4, shard % 4
    ahead = 1 - 2 * c
    rows, ff = anchor.shape

    early = jnp.stack([(y + 2) % 4, (y - ahead) % 4])
    late = jnp.stack([(y + ahead) % 4, y])
    both = jnp.concatenate([early, late])
    pass_on, keep = (zl ^ 2) * 4, zl * 4

    blocks = pseudo_grad[0].reshape(4, 4 * rows, ff)
    from_core = send(half_of(blocks, 1 - c), CORE)
    base = anchor - (outer_rate * momentum_decay * momentum_decay) * momentum
    base_core = send(half_of(base, 1 - c), CORE)
    base = by_index(c, half_of(base, c), base_core)

    no_blocks = jnp.zeros((0,), jnp.int32)
    far_f1 = send(pack(cotangent, tokens, None, (3 - zl) * 4 + early), ZL1)

    total = half_of(blocks, c).astype(f32) + from_core.astype(f32)
    got = [send(pick(total, (x + d) % 4).astype(bf16), x_by(d)) for d in (1, 2, 3)]
    total = pick(total, x)
    for part in got:
        total = total + part.astype(f32)
    total = total.reshape(2, 2, rows, HALF)
    got = send(gate(pick(total, 1 - zh).astype(bf16), far_f1), ZH)
    mean_delta = (pick(total, zh) + got.astype(f32)) / replicas
    weight = base - (outer_rate * (1 + momentum_decay)) * mean_delta
    weight = weight.astype(bf16)
    weight = by_index(zh, weight, send(weight, ZH)).reshape(4 * rows, HALF)

    got = [send(weight, zl_by(d)) for d in (1, 2, 3)]
    weight = ring_stack([weight[None], *[g[None] for g in got]], [zl, zl - 1, zl - 2, zl - 3])[0]
    other_tokens = send(tokens, CORE)
    z_2_in = pack(cotangent, tokens, (0, HALF), (3 - zl) * 4 + late, weight)
    z_2 = send(z_2_in, ZL1)
    got = [send(weight, y_by(d)) for d in (2, 1, -1)]
    weight = ring_stack([weight, *got], [y, y - 2, y - 1, y + 1]).reshape(1024, HALF)
    xa = send(weight, X_AHEAD)
    xb = send(weight, X_BACK)
    cot_1 = send(pack(cotangent, tokens, (HALF, HALF), no_blocks, weight), ZL1)
    far_o = send(pack(cotangent, tokens, None, (zl ^ 1) * 4 + both, weight), ZL1)
    xr_in = gate(xa, xb)
    xr = send(xr_in, X_AHEAD)

    delta_core = send(pick(mean_delta, 1 - c), CORE)
    delta = by_index(c, pick(mean_delta, c), delta_core)
    delta = jnp.concatenate([delta[0], delta[1]], axis=1)
    moment_out = momentum_decay * momentum + delta
    anchor_out = anchor - outer_rate * (delta + momentum_decay * moment_out)

    def ring_sum(block, got):
        return block + got.astype(f32)

    kinds = (bf16, bf16, f32, f32)
    first, second = (far_f1, 0, 512), (z_2, 0, HALF + 512)
    f_0 = terms(pass_on + both, tokens, [first, second], cotangent, 0, [(z_2, 0)], factor, kinds, weight)
    u_a = send(f_0[0], Y_AHEAD)
    u_b = send(f_0[1], Y_BACK)
    u_c = send(ring_sum(f_0[2], u_a).astype(bf16), Y_AHEAD)
    last_0 = send(ring_sum(ring_sum(f_0[3], u_b), u_c).astype(bf16), ZL2)
    f_1 = terms(pass_on + both, tokens, [first, second], cotangent, 1, [(cot_1, 0)], factor, kinds, f_0[3])
    v_a = send(f_1[0], Y_AHEAD)
    v_b = send(f_1[1], Y_BACK)
    v_c = send(ring_sum(f_1[2], v_a).astype(bf16), Y_AHEAD)
    last_1 = send(ring_sum(ring_sum(f_1[3], v_b), v_c).astype(bf16), ZL2)
    cots = [(z_2, 0), (cot_1, 0)]
    o = terms(keep + both, tokens, [(far_o, 0, 1024)], cotangent, 0, cots, factor, kinds, f_1[3], xr_in)
    w_a = send(o[0], Y_AHEAD)
    w_b = send(o[1], Y_BACK)
    w_c = send(gate(ring_sum(o[2], w_a).astype(bf16), last_0), Y_AHEAD)

    act, back = activations(
        tokens, other_tokens, [weight, xr_in, xb, xr], [x, x - ahead, x + ahead, x + 2], factor, o[3]
    )
    back = send(back, CORE)
    up_acts = jnp.where(
        c == 0, jnp.concatenate([act, back], axis=1), jnp.concatenate([back, act], axis=1)
    )
    grad = ring_sum(ring_sum(o[3], w_b), w_c)
    grad = ring_sum(grad, jnp.concatenate([last_0, last_1], axis=1))
    return (anchor_out, moment_out, up_acts, grad.astype(bf16)[None])


def solution(mesh):
    in_specs = (
        P(("replica", "shard"), None),
        P(("replica", "shard"), None),
        P("replica", "shard", None),
        P(("shard", "replica"), None),
        P(("shard", "replica"), None),
    )
    out_specs = (
        P(("shard", "replica"), None),
        P(("shard", "replica"), None),
        P(("replica", "shard"), None),
        P("replica", "shard", None),
    )
    return jax.shard_map(
        on_device, mesh=mesh, in_specs=in_specs, out_specs=out_specs, check_vma=False
    )
```

time: 624 us -> 217 us (0.35)
  waiting for transfers between devices: 533 us -> 77.7 us
  starting transfers between devices: 0.12 us -> 61 us
  Pallas kernels: 0 us -> 55.4 us
  blocking collectives: 36.2 us -> 0 us
  matrix products: 29.9 us -> 0 us
  between operations: 13.8 us -> 1.01 us
  other arithmetic: 6.79 us -> 14.1 us
    reduce_scatter x2 -> x0, waiting for transfers between devices: 387 us -> none  [the longest x1 297 us: on_device(): lax.psum_scatter(lax.dot_general(columns, cotangent, (((0,), (0,)), ((),...]
    all_gather x1 -> x0, waiting for transfers between devices: 146 us -> none  [on_device(): lax.all_gather(group_rows, 'shard', axis=0, tiled=True)]
    ppermute x0 -> x34, waiting for transfers between devices: none -> 77.7 us  [send(): return lax.ppermute(array, AXES, pairs)]
    ppermute x0 -> x34, starting transfers between devices: none -> 61 us  [send(): return lax.ppermute(array, AXES, pairs)]
    pallas_call x0 -> x13, Pallas kernels: none -> 55.4 us  [the longest x3 23.5 us: terms(): pl.pallas_call(functools.partial(term_body, factor, (count, len(fars), tu...]
    all_gather x1 -> x0, blocking collectives: 36.2 us -> none  [on_device(): lax.all_gather(anchor_out.astype(jnp.bfloat16), 'replica', axis=0, tiled=...]
    dot_general x2 -> x0, matrix products: 29.9 us -> none  [the longest x1 16.6 us: on_device(): lax.dot_general(columns, cotangent, (((0,), (0,)), ((), ())), preferred_e...]
  transfers between devices with their start and end apart: 3 -> 34, of which waited for: 3 -> 14; matrix products, arithmetic and copies ran while one was open for 5% -> 6% of each run, Pallas kernels for 0% -> 22%
where the time goes in v1:
time: 217 us; the launch traced here: 216 us
  waiting for transfers between devices  77.7 us (36%)
  starting transfers between devices  61 us (28%)
  Pallas kernels  55.4 us (26%)
  other arithmetic  14.1 us (6%)
  local copies, waits for them, and re-layouts  7.15 us (3%)
    ppermute x34, waiting for transfers between devices, send(): return lax.ppermute(array, AXES, pairs)  77.7 us
    ppermute x34, starting transfers between devices, send(): return lax.ppermute(array, AXES, pairs)  61 us
    pallas_call x3, Pallas kernels, terms(): pl.pallas_call(functools.partial(term_body, factor, (count, len(fars), tu...  23.5 us
    pallas_call x1, Pallas kernels, activations(): pl.pallas_call(functools.partial(act_body, factor), grid_spec=pltpu.Prefe...  16.3 us
    pallas_call x4, Pallas kernels, pack(): pl.pallas_call(functools.partial(pack_body, width, count), grid_spec=pltp...  10.9 us
    unnamed x60, local copies, waits for them, and re-layouts  6.46 us
    pallas_call x2, Pallas kernels, ring_stack(): pl.pallas_call(functools.partial(stack_body, len(parts)), in_specs=[pl.Bl...  4.69 us
  transfers between devices with their start and end apart: 34, of which 14 were waited for; matrix products, arithmetic and copies ran while one was open for 6% of the time, Pallas kernels for 22%

profile of v1, /device:TPU:1, one launch (start us, length us, event | category | flops | bytes accessed | tf_op | source)
XLA Modules:
  0.0 216.3 jit_solution(6613804345621865357)
XLA Ops:
  1.3 2.7 %shard_map.84 = bf16[512,512]{1,0:T(8,128)(2,1)} custom-call(s32[2]{0:T(128)} %add_add_fusion.at, bf16[512,1792]{1,0:T(8,128)(2,1)} %refs_5_.1, bf16[512,4096]{1,0:T(8,128)(2,1)} %mine.1, bf16[512,4096]{1,0:T(8,128)(2,1)} %mine.1), custom_call_target="tpu_custom_call" | custom-call | tf_op jit(solution)/shard_map/pallas_call | solution.py:129
  4.0 2.5 %collective-permute-start.4 = (bf16[512,512]{1,0:T(8,128)(2,1)}, bf16[512,512]{1,0:T(8,128)(2,1)S(1)}, u32[]{:S(2)}, u32[]{:S(2)}) collective-permute-start(bf16[512,512]{1,0:T(8,128)(2,1)} %shard_map.84), channel_id=1, source_target_pairs={{0,4},{1,5},{2,6},{3,7},{4,0},{5,1},{6,2},{7,3},{8,12},{9,13},{10,... | collective-permute-start | bytes 1572872 | tf_op jit(solution)/shard_map/ppermute | solution.py:58
  7.6 1.4 collective-permute-done
  9.2 1.3 collective-permute-start.1
  10.5 2.5 %collective-permute-start.2 = (bf16[64,896]{1,0:T(8,128)(2,1)S(1)}, bf16[64,896]{1,0:T(8,128)(2,1)S(1)}, u32[]{:S(2)}, u32[]{:S(2)}) collective-permute-start(bf16[64,896]{1,0:T(8,128)(2,1)S(1)} %get-tuple-element.38), channel_id=1, source_target_pairs={{0,128},{1,129},{2,130},{3,131},{4,132},{5,133},{6,134},{7,135},{8... | collective-permute-start | bytes 344072 | tf_op jit(solution)/shard_map/ppermute | solution.py:58
  13.0 1.2 collective-permute-start.3
  14.1 1.3 collective-permute-start.8
  15.4 2.9 %collective-permute-done.2 = bf16[64,896]{1,0:T(8,128)(2,1)S(1)} collective-permute-done((bf16[64,896]{1,0:T(8,128)(2,1)S(1)}, bf16[64,896]{1,0:T(8,128)(2,1)S(1)}, u32[]{:S(2)}, u32[]{:S(2)}) %collective-permute-start.2) | collective-permute-done | bytes 114720 | tf_op jit(solution)/shard_map/ppermute | solution.py:58
  19.8 6.0 %collective-permute-start.5 = (bf16[2,16,896]{2,1,0:T(8,128)(2,1)}, bf16[2,16,896]{2,1,0:T(8,128)(2,1)S(1)}, u32[]{:S(2)}, u32[]{:S(2)}) collective-permute-start(bf16[2,16,896]{2,1,0:T(8,128)(2,1)} %shard_map.85), channel_id=1, source_target_pairs={{0,32},{1,33},{2,34},{3,35},{4,36},{5,37},{6,38},{7,39},{8,40},{9,... | collective-permute-start | bytes 172040 | tf_op jit(solution)/shard_map/ppermute | solution.py:58
  25.9 2.1 collective-permute-done.5
  28.0 5.9 %collective-permute-start.9 = (bf16[2,16,896]{2,1,0:T(8,128)(2,1)S(1)}, bf16[2,16,896]{2,1,0:T(8,128)(2,1)S(1)}, u32[]{:S(2)}, u32[]{:S(2)}) collective-permute-start(bf16[2,16,896]{2,1,0:T(8,128)(2,1)S(1)} %get-tuple-element.39), channel_id=1, source_target_pairs={{0,32},{1,33},{2,34},{3,35},{4,36},{5,37},{6,38},{7,39},{8,40},{9,... | collective-permute-start | bytes 172040 | tf_op jit(solution)/shard_map/ppermute | solution.py:58
  33.8 1.7 collective-permute-done.9
  35.6 2.8 %collective-permute-start.11 = (bf16[64,896]{1,0:T(8,128)(2,1)S(1)}, bf16[64,896]{1,0:T(8,128)(2,1)S(1)}, u32[]{:S(2)}, u32[]{:S(2)}) collective-permute-start(bf16[64,896]{1,0:T(8,128)(2,1)S(1)} %bitcast.75), channel_id=1, source_target_pairs={{0,8},{1,9},{2,10},{3,11},{4,12},{5,13},{6,14},{7,15},{8,0},{9,1},... | collective-permute-start | bytes 344072 | tf_op jit(solution)/shard_map/ppermute | solution.py:58
  38.4 2.3 %collective-permute-start.12 = (bf16[64,896]{1,0:T(8,128)(2,1)S(1)}, bf16[64,896]{1,0:T(8,128)(2,1)S(1)}, u32[]{:S(2)}, u32[]{:S(2)}) collective-permute-start(bf16[64,896]{1,0:T(8,128)(2,1)S(1)} %bitcast.76), channel_id=1, source_target_pairs={{0,12},{1,13},{2,14},{3,15},{4,0},{5,1},{6,2},{7,3},{8,4},{9,5},{1... | collective-permute-start | bytes 344072 | tf_op jit(solution)/shard_map/ppermute | solution.py:58
  43.7 1.9 shard_map.86
  45.6 3.1 %shard_map.90 = bf16[512,1408]{1,0:T(8,128)(2,1)} custom-call(s32[2]{0:T(128)} %add_add_fusion.1.at, bf16[512,1792]{1,0:T(8,128)(2,1)} %refs_5_.1, bf16[512,4096]{1,0:T(8,128)(2,1)} %mine.1, bf16[512,4096]{1,0:T(8,128)(2,1)} %mine.1, bf16[4,64,896]{2,1,0:T(8,128)(2,1)} %bitcast.65), custom_call_target="tpu_custom_call" | custom-call | tf_op jit(solution)/shard_map/pallas_call | solution.py:129
  48.7 4.7 %collective-permute-start.20 = (bf16[512,1408]{1,0:T(8,128)(2,1)}, bf16[512,1408]{1,0:T(8,128)(2,1)S(1)}, u32[]{:S(2)}, u32[]{:S(2)}) collective-permute-start(bf16[512,1408]{1,0:T(8,128)(2,1)} %shard_map.90), channel_id=1, source_target_pairs={{0,4},{1,5},{2,6},{3,7},{4,0},{5,1},{6,2},{7,3},{8,12},{9,13},{10,... | collective-permute-start | bytes 4325384 | tf_op jit(solution)/shard_map/ppermute | solution.py:58
  53.4 2.9 %collective-permute-start.13 = (bf16[4,64,896]{2,1,0:T(8,128)(2,1)S(1)}, bf16[4,64,896]{2,1,0:T(8,128)(2,1)S(1)}, u32[]{:S(2)}, u32[]{:S(2)}) collective-permute-start(bf16[4,64,896]{2,1,0:T(8,128)(2,1)S(1)} %bitcast.67), channel_id=1, source_target_pairs={{0,2},{1,3},{2,0},{3,1},{4,6},{5,7},{6,4},{7,5},{8,10},{9,11},{10,... | collective-permute-start | bytes 1376264 | tf_op jit(solution)/shard_map/ppermute | solution.py:58
  56.7 2.3 %collective-permute-start.15 = (bf16[4,64,896]{2,1,0:T(8,128)(2,1)S(1)}, bf16[4,64,896]{2,1,0:T(8,128)(2,1)S(1)}, u32[]{:S(2)}, u32[]{:S(2)}) collective-permute-start(bf16[4,64,896]{2,1,0:T(8,128)(2,1)S(1)} %bitcast.69), channel_id=1, source_target_pairs={{0,3},{1,0},{2,1},{3,2},{4,7},{5,4},{6,5},{7,6},{8,11},{9,8},{10,9... | collective-permute-start | bytes 1376264 | tf_op jit(solution)/shard_map/ppermute | solution.py:58
  59.0 3.5 %collective-permute-start.7 = (bf16[512,4096]{1,0:T(8,128)(2,1)}, bf16[512,4096]{1,0:T(8,128)(2,1)}, u32[]{:S(2)}, u32[]{:S(2)}) collective-permute-start(bf16[512,4096]{1,0:T(8,128)(2,1)} %mine.1), channel_id=1, source_target_pairs={{0,16},{1,17},{2,18},{3,19},{4,20},{5,21},{6,22},{7,23},{8,24},{9,... | collective-permute-start | bytes 12582920 | tf_op jit(solution)/shard_map/ppermute | solution.py:58
  64.3 12.9 %collective-permute-done.14.refs_2_ = bf16[4,64,896]{2,1,0:T(8,128)(2,1)S(1)} collective-permute-done((bf16[4,64,896]{2,1,0:T(8,128)(2,1)S(1)}, bf16[4,64,896]{2,1,0:T(8,128)(2,1)S(1)}, u32[]{:S(2)}, u32[]{:S(2)}) %collective-permute-start.14) | collective-permute-done | bytes 458784 | tf_op jit(solution)/shard_map/ppermute | solution.py:58
  78.7 2.8 %shard_map.87 = bf16[4,4,64,896]{3,2,1,0:T(8,128)(2,1)} custom-call(s32[4]{0:T(128)} %and_select_fusion.1.at, bf16[4,64,896]{2,1,0:T(8,128)(2,1)} %bitcast.66, bf16[4,64,896]{2,1,0:T(8,128)(2,1)} %copy-done.19, bf16[4,64,896]{2,1,0:T(8,128)(2,1)} %copy-done.20, bf16[4,64,896]{2,1,0:T(8,128)(2,1)} %copy-done.21), custom_call_target="tpu_custom_call" | custom-call | tf_op jit(solution)/shard_map/pallas_call | solution.py:98
  81.5 2.2 %collective-permute-start.16 = (bf16[1024,896]{1,0:T(8,128)(2,1)}, bf16[1024,896]{1,0:T(8,128)(2,1)S(1)}, u32[]{:S(2)}, u32[]{:S(2)}) collective-permute-start(bf16[1024,896]{1,0:T(8,128)(2,1)} %bitcast.59), channel_id=1, source_target_pairs={{0,64},{1,65},{2,66},{3,67},{4,68},{5,69},{6,70},{7,71},{8,72},{9,... | collective-permute-start | bytes 5505032 | tf_op jit(solution)/shard_map/ppermute | solution.py:58
  84.4 1.2 copy-done
  85.5 6.9 %shard_map.92 = (bf16[256,896]{1,0:T(8,128)(2,1)}, bf16[256,896]{1,0:T(8,128)(2,1)}, f32[256,896]{1,0:T(8,128)}, f32[256,896]{1,0:T(8,128)}) custom-call(s32[4]{0:T(128)} %get-tuple-element.32.at, bf16[512,4096]{1,0:T(8,128)(2,1)} %mine.1, bf16[512,4096]{1,0:T(8,128)(2,1)} %mine.1, bf16[512,4096]{1,0:T(8,128)(2,1)} %mine.1, bf16[512,4096]{1,0:T(8,128)(2,1)} %mine.1, ...), custom_call_target="tpu_custom_call" | custom-call | tf_op jit(solution)/shard_map/pallas_call | solution.py:177
  92.5 1.8 collective-permute-start.26
  94.3 2.0 shard_map.91
  97.7 3.0 %shard_map.89 = bf16[512,1024]{1,0:T(8,128)(2,1)} custom-call(s32[4]{0:T(128)} %get-tuple-element.47.at, bf16[512,1792]{1,0:T(8,128)(2,1)} %refs_5_.1, bf16[512,4096]{1,0:T(8,128)(2,1)} %mine.1, bf16[512,4096]{1,0:T(8,128)(2,1)} %mine.1, bf16[512,4096]{1,0:T(8,128)(2,1)} %mine.1, bf16[512,4096]{1,0:T(8,128)(2,1)} %mine.1, bf16[1024,896]{1,0:T(8,128)(2,1)} %bitcast.63), custom_call_target="tpu_custom_call" | custom-call | tf_op jit(solution)/shard_map/pallas_call | solution.py:129
  101.5 15.5 %collective-permute-done.21.refs_7_ = bf16[512,896]{1,0:T(8,128)(2,1)S(1)} collective-permute-done((bf16[512,896]{1,0:T(8,128)(2,1)}, bf16[512,896]{1,0:T(8,128)(2,1)S(1)}, u32[]{:S(2)}, u32[]{:S(2)}) %collective-permute-start.21) | collective-permute-done | bytes 917536 | tf_op jit(solution)/shard_map/ppermute | solution.py:58
  116.9 5.3 %collective-permute-done.16.refs_0_ = bf16[1024,896]{1,0:T(8,128)(2,1)S(1)} collective-permute-done((bf16[1024,896]{1,0:T(8,128)(2,1)}, bf16[1024,896]{1,0:T(8,128)(2,1)S(1)}, u32[]{:S(2)}, u32[]{:S(2)}) %collective-permute-start.16) | collective-permute-done | bytes 1835040 | tf_op jit(solution)/shard_map/ppermute | solution.py:58
  122.2 1.7 collective-permute-start.27
  123.9 6.8 %shard_map.93 = (bf16[256,896]{1,0:T(8,128)(2,1)}, bf16[256,896]{1,0:T(8,128)(2,1)}, f32[256,896]{1,0:T(8,128)}, f32[256,896]{1,0:T(8,128)}) custom-call(s32[4]{0:T(128)} %get-tuple-element.32.at, bf16[512,4096]{1,0:T(8,128)(2,1)} %mine.1, bf16[512,4096]{1,0:T(8,128)(2,1)} %mine.1, bf16[512,4096]{1,0:T(8,128)(2,1)} %mine.1, bf16[512,4096]{1,0:T(8,128)(2,1)} %mine.1, ...), custom_call_target="tpu_custom_call" | custom-call | tf_op jit(solution)/shard_map/pallas_call | solution.py:177
  130.7 8.6 %collective-permute-done.19.refs_4_ = bf16[512,1024]{1,0:T(8,128)(2,1)S(1)} collective-permute-done((bf16[512,1024]{1,0:T(8,128)(2,1)}, bf16[512,1024]{1,0:T(8,128)(2,1)S(1)}, u32[]{:S(2)}, u32[]{:S(2)}) %collective-permute-start.19) | collective-permute-done | bytes 1048608 | tf_op jit(solution)/shard_map/ppermute | solution.py:58
  140.3 9.8 %shard_map.94 = (bf16[256,1792]{1,0:T(8,128)(2,1)}, bf16[256,1792]{1,0:T(8,128)(2,1)}, f32[256,1792]{1,0:T(8,128)}, f32[256,1792]{1,0:T(8,128)}) custom-call(s32[4]{0:T(128)} %get-tuple-element.48.at, bf16[512,4096]{1,0:T(8,128)(2,1)} %mine.1, bf16[512,4096]{1,0:T(8,128)(2,1)} %mine.1, bf16[512,4096]{1,0:T(8,128)(2,1)} %mine.1, bf16[512,4096]{1,0:T(8,128)(2,1)} %mine.1, ...), custom_call_target="tpu_custom_call" | custom-call | tf_op jit(solution)/shard_map/pallas_call | solution.py:177
  150.2 3.3 %collective-permute-start.18 = (bf16[1024,896]{1,0:T(8,128)(2,1)S(1)}, bf16[1024,896]{1,0:T(8,128)(2,1)S(1)}, u32[]{:S(2)}, u32[]{:S(2)}) collective-permute-start(bf16[1024,896]{1,0:T(8,128)(2,1)S(1)} %copy-done.2), channel_id=1, source_target_pairs={{0,64},{1,65},{2,66},{3,67},{4,68},{5,69},{6,70},{7,71},{8,72},{9,... | collective-permute-start | bytes 5505032 | tf_op jit(solution)/shard_map/ppermute | solution.py:58
  153.6 1.3 add_convert_fusion.4
  155.6 12.2 %collective-permute-done.31 = bf16[256,896]{1,0:T(8,128)(2,1)S(1)} collective-permute-done((bf16[256,896]{1,0:T(8,128)(2,1)}, bf16[256,896]{1,0:T(8,128)(2,1)S(1)}, u32[]{:S(2)}, u32[]{:S(2)}) %collective-permute-start.31) | collective-permute-done | bytes 458784 | tf_op jit(solution)/shard_map/ppermute | solution.py:58
  167.7 4.5 %collective-permute-start.6 = (f32[16,896]{1,0:T(8,128)S(1)}, f32[16,896]{1,0:T(8,128)S(1)}, u32[]{:S(2)}, u32[]{:S(2)}) collective-permute-start(f32[16,896]{1,0:T(8,128)S(1)} %dynamic-slice_bitcast_fusion), channel_id=1, source_target_pairs={{0,16},{1,17},{2,18},{3,19},{4,20},{5,21},{6,22},{7,23},{8,24},{9,... | collective-permute-start | bytes 172040 | tf_op jit(solution)/shard_map/ppermute | solution.py:58
  172.3 4.9 %collective-permute-done.28.refs_1_ = bf16[256,896]{1,0:T(8,128)(2,1)S(1)} collective-permute-done((bf16[256,896]{1,0:T(8,128)(2,1)S(1)}, bf16[256,896]{1,0:T(8,128)(2,1)S(1)}, u32[]{:S(2)}, u32[]{:S(2)}) %collective-permute-start.28) | collective-permute-done | bytes 458784 | tf_op jit(solution)/shard_map/ppermute | solution.py:58
  177.3 1.4 collective-permute-start.30
  178.7 1.3 collective-permute-start.32
  179.9 2.3 %add_convert_fusion.1.refs_0_ = bf16[256,1792]{1,0:T(8,128)(2,1)} fusion(f32[256,1792]{1,0:T(8,128)S(1)} %copy-done.11, bf16[256,1792]{1,0:T(8,128)(2,1)} %collective-permute-done.24), kind=kLoop, calls=%fused_computation.2 | loop fusion | flops 1376256 | bytes 3670016 | tf_op jit(solution)/shard_map/convert_element_type | solution.py:324
  182.5 7.4 %collective-permute-done.30 = bf16[256,896]{1,0:T(8,128)(2,1)S(1)} collective-permute-done((bf16[256,896]{1,0:T(8,128)(2,1)}, bf16[256,896]{1,0:T(8,128)(2,1)S(1)}, u32[]{:S(2)}, u32[]{:S(2)}) %collective-permute-start.30) | collective-permute-done | bytes 458784 | tf_op jit(solution)/shard_map/ppermute | solution.py:58
  191.5 1.3 copy-done.10
  192.7 16.3 %shard_map.95 = (bf16[512,896]{1,0:T(8,128)(2,1)}, bf16[512,896]{1,0:T(8,128)(2,1)}) custom-call(s32[4]{0:T(128)} %and_select_fusion.2.at, bf16[512,4096]{1,0:T(8,128)(2,1)} %mine.1, bf16[512,4096]{1,0:T(8,128)(2,1)} %collective-permute-done.7.other, bf16[1024,896]{1,0:T(8,128)(2,1)} %bitcast.64, bf16[1024,896]{1,0:T(8,128)(2,1)} %shard_map.88.refs_9_.refs_1_, ...), custom_call_target="tpu_custom_call" | custom-call | tf_op jit(solution)/shard_map/pallas_call | solution.py:231
  209.1 2.2 %collective-permute-start.22 = (bf16[512,896]{1,0:T(8,128)(2,1)}, bf16[512,896]{1,0:T(8,128)(2,1)S(1)}, u32[]{:S(2)}, u32[]{:S(2)}) collective-permute-start(bf16[512,896]{1,0:T(8,128)(2,1)} %get-tuple-element.22), channel_id=1, source_target_pairs={{0,16},{1,17},{2,18},{3,19},{4,20},{5,21},{6,22},{7,23},{8,24},{9,... | collective-permute-start | bytes 2752520 | tf_op jit(solution)/shard_map/ppermute | solution.py:58
  212.1 2.6 %fusion = bf16[1,256,1792]{2,1,0:T(8,128)(2,1)} fusion(bf16[256,1792]{1,0:T(8,128)(2,1)} %collective-permute-done.29, f32[256,1792]{1,0:T(8,128)S(1)} %copy-done.3, bf16[256,1792]{1,0:T(8,128)(2,1)S(1)} %collective-permute-done.23, bf16[256,896]{1,0:T(8,128)(2,1)S(1)} %collective-permute-done.33, bf16[256,896]{1,0:T(8,128)(2,1)S(1)} %copy-done.13), kind=kLoop, calls=%fused_computation.3 | loop fusion | flops 4587520 | bytes 5505024 | tf_op jit(solution)/shard_map/broadcast_in_dim | solution.py:335
  214.6 1.6 maximum_select_fusion
  (121 shorter events, 17.5 us)
Async XLA Ops:
  4.0 15.0 %collective-permute-start.4 = (bf16[512,512]{1,0:T(8,128)(2,1)}, bf16[512,512]{1,0:T(8,128)(2,1)S(1)}, u32[]{:S(2)}, u32[]{:S(2)}) collective-permute-start(bf16[512,512]{1,0:T(8,128)(2,1)} %shard_map.84), channel_id=1, source_target_pairs={{0,4},{1,5},{2,6},{3,7},{4,0},{5,1},{6,2},{7,3},{8,12},{9,13},{10,... | collective-permute-start | bytes 1572872 | tf_op jit(solution)/shard_map/ppermute | solution.py:58
  6.5 2.5 %collective-permute-start = (bf16[4,64,896]{2,1,0:T(8,128)(2,1)S(1)}, bf16[4,64,896]{2,1,0:T(8,128)(2,1)S(1)}, u32[]{:S(2)}, u32[]{:S(2)}) collective-permute-start(bf16[4,64,896]{2,1,0:T(8,128)(2,1)S(1)} %broadcast_select_fusion), channel_id=1, source_target_pairs={{0,16},{1,17},{2,18},{3,19},{4,20},{5,21},{6,22},{7,23},{8,24},{9,... | collective-permute-start | bytes 1376264 | tf_op jit(solution)/shard_map/ppermute | solution.py:58
  9.2 6.2 %collective-permute-start.1 = (bf16[64,896]{1,0:T(8,128)(2,1)S(1)}, bf16[64,896]{1,0:T(8,128)(2,1)S(1)}, u32[]{:S(2)}, u32[]{:S(2)}) collective-permute-start(bf16[64,896]{1,0:T(8,128)(2,1)S(1)} %get-tuple-element.36), channel_id=1, source_target_pairs={{0,64},{1,65},{2,66},{3,67},{4,68},{5,69},{6,70},{7,71},{8,72},{9,... | collective-permute-start | bytes 344072 | tf_op jit(solution)/shard_map/ppermute | solution.py:58
  10.5 7.8 %collective-permute-start.2 = (bf16[64,896]{1,0:T(8,128)(2,1)S(1)}, bf16[64,896]{1,0:T(8,128)(2,1)S(1)}, u32[]{:S(2)}, u32[]{:S(2)}) collective-permute-start(bf16[64,896]{1,0:T(8,128)(2,1)S(1)} %get-tuple-element.38), channel_id=1, source_target_pairs={{0,128},{1,129},{2,130},{3,131},{4,132},{5,133},{6,134},{7,135},{8... | collective-permute-start | bytes 344072 | tf_op jit(solution)/shard_map/ppermute | solution.py:58
  13.0 5.4 %collective-permute-start.3 = (bf16[64,896]{1,0:T(8,128)(2,1)S(1)}, bf16[64,896]{1,0:T(8,128)(2,1)S(1)}, u32[]{:S(2)}, u32[]{:S(2)}) collective-permute-start(bf16[64,896]{1,0:T(8,128)(2,1)S(1)} %get-tuple-element.37), channel_id=1, source_target_pairs={{0,192},{1,193},{2,194},{3,195},{4,196},{5,197},{6,198},{7,199},{8... | collective-permute-start | bytes 344072 | tf_op jit(solution)/shard_map/ppermute | solution.py:58
  14.1 11.7 %collective-permute-start.8 = (f32[16,896]{1,0:T(8,128)S(1)}, f32[16,896]{1,0:T(8,128)S(1)}, u32[]{:S(2)}, u32[]{:S(2)}) collective-permute-start(f32[16,896]{1,0:T(8,128)S(1)} %slice_select_fusion), channel_id=1, source_target_pairs={{0,16},{1,17},{2,18},{3,19},{4,20},{5,21},{6,22},{7,23},{8,24},{9,... | collective-permute-start | bytes 172040 | tf_op jit(solution)/shard_map/ppermute | solution.py:58
  19.8 8.1 %collective-permute-start.5 = (bf16[2,16,896]{2,1,0:T(8,128)(2,1)}, bf16[2,16,896]{2,1,0:T(8,128)(2,1)S(1)}, u32[]{:S(2)}, u32[]{:S(2)}) collective-permute-start(bf16[2,16,896]{2,1,0:T(8,128)(2,1)} %shard_map.85), channel_id=1, source_target_pairs={{0,32},{1,33},{2,34},{3,35},{4,36},{5,37},{6,38},{7,39},{8,40},{9,... | collective-permute-start | bytes 172040 | tf_op jit(solution)/shard_map/ppermute | solution.py:58
  28.0 7.5 %collective-permute-start.9 = (bf16[2,16,896]{2,1,0:T(8,128)(2,1)S(1)}, bf16[2,16,896]{2,1,0:T(8,128)(2,1)S(1)}, u32[]{:S(2)}, u32[]{:S(2)}) collective-permute-start(bf16[2,16,896]{2,1,0:T(8,128)(2,1)S(1)} %get-tuple-element.39), channel_id=1, source_target_pairs={{0,32},{1,33},{2,34},{3,35},{4,36},{5,37},{6,38},{7,39},{8,40},{9,... | collective-permute-start | bytes 172040 | tf_op jit(solution)/shard_map/ppermute | solution.py:58
  35.5 7.5 %copy-start.18 = (bf16[2,2,16,896]{3,2,1,0:T(8,128)(2,1)}, bf16[2,2,16,896]{3,2,1,0:T(8,128)(2,1)S(1)}, u32[]{:S(2)}) copy-start(bf16[2,2,16,896]{3,2,1,0:T(8,128)(2,1)S(1)} %pad_maximum_fusion.1) | copy-start | bytes 344068
  35.5 6.4 %collective-permute-start.10 = (bf16[64,896]{1,0:T(8,128)(2,1)S(1)}, bf16[64,896]{1,0:T(8,128)(2,1)S(1)}, u32[]{:S(2)}, u32[]{:S(2)}) collective-permute-start(bf16[64,896]{1,0:T(8,128)(2,1)S(1)} %bitcast.74), channel_id=1, source_target_pairs={{0,4},{1,5},{2,6},{3,7},{4,8},{5,9},{6,10},{7,11},{8,12},{9,13},{1... | collective-permute-start | bytes 344072 | tf_op jit(solution)/shard_map/ppermute | solution.py:58
  35.6 7.4 %collective-permute-start.11 = (bf16[64,896]{1,0:T(8,128)(2,1)S(1)}, bf16[64,896]{1,0:T(8,128)(2,1)S(1)}, u32[]{:S(2)}, u32[]{:S(2)}) collective-permute-start(bf16[64,896]{1,0:T(8,128)(2,1)S(1)} %bitcast.75), channel_id=1, source_target_pairs={{0,8},{1,9},{2,10},{3,11},{4,12},{5,13},{6,14},{7,15},{8,0},{9,1},... | collective-permute-start | bytes 344072 | tf_op jit(solution)/shard_map/ppermute | solution.py:58
  38.4 4.6 %collective-permute-start.12 = (bf16[64,896]{1,0:T(8,128)(2,1)S(1)}, bf16[64,896]{1,0:T(8,128)(2,1)S(1)}, u32[]{:S(2)}, u32[]{:S(2)}) collective-permute-start(bf16[64,896]{1,0:T(8,128)(2,1)S(1)} %bitcast.76), channel_id=1, source_target_pairs={{0,12},{1,13},{2,14},{3,15},{4,0},{5,1},{6,2},{7,3},{8,4},{9,5},{1... | collective-permute-start | bytes 344072 | tf_op jit(solution)/shard_map/ppermute | solution.py:58
  45.6 7.8 %copy-start.5 = (bf16[1,4,64,896]{3,2,1,0:T(8,128)(2,1)S(1)}, bf16[1,4,64,896]{3,2,1,0:T(8,128)(2,1)}, u32[]{:S(2)}) copy-start(bf16[1,4,64,896]{3,2,1,0:T(8,128)(2,1)} %shard_map.86) | copy-start | bytes 1376260
  48.7 35.6 %collective-permute-start.20 = (bf16[512,1408]{1,0:T(8,128)(2,1)}, bf16[512,1408]{1,0:T(8,128)(2,1)S(1)}, u32[]{:S(2)}, u32[]{:S(2)}) collective-permute-start(bf16[512,1408]{1,0:T(8,128)(2,1)} %shard_map.90), channel_id=1, source_target_pairs={{0,4},{1,5},{2,6},{3,7},{4,0},{5,1},{6,2},{7,3},{8,12},{9,13},{10,... | collective-permute-start | bytes 4325384 | tf_op jit(solution)/shard_map/ppermute | solution.py:58
  53.4 10.9 %collective-permute-start.13 = (bf16[4,64,896]{2,1,0:T(8,128)(2,1)S(1)}, bf16[4,64,896]{2,1,0:T(8,128)(2,1)S(1)}, u32[]{:S(2)}, u32[]{:S(2)}) collective-permute-start(bf16[4,64,896]{2,1,0:T(8,128)(2,1)S(1)} %bitcast.67), channel_id=1, source_target_pairs={{0,2},{1,3},{2,0},{3,1},{4,6},{5,7},{6,4},{7,5},{8,10},{9,11},{10,... | collective-permute-start | bytes 1376264 | tf_op jit(solution)/shard_map/ppermute | solution.py:58
  56.3 20.9 %collective-permute-start.14 = (bf16[4,64,896]{2,1,0:T(8,128)(2,1)S(1)}, bf16[4,64,896]{2,1,0:T(8,128)(2,1)S(1)}, u32[]{:S(2)}, u32[]{:S(2)}) collective-permute-start(bf16[4,64,896]{2,1,0:T(8,128)(2,1)S(1)} %bitcast.68), channel_id=1, source_target_pairs={{0,1},{1,2},{2,3},{3,0},{4,5},{5,6},{6,7},{7,4},{8,9},{9,10},{10,1... | collective-permute-start | bytes 1376264 | tf_op jit(solution)/shard_map/ppermute | solution.py:58
  56.7 20.5 %collective-permute-start.15 = (bf16[4,64,896]{2,1,0:T(8,128)(2,1)S(1)}, bf16[4,64,896]{2,1,0:T(8,128)(2,1)S(1)}, u32[]{:S(2)}, u32[]{:S(2)}) collective-permute-start(bf16[4,64,896]{2,1,0:T(8,128)(2,1)S(1)} %bitcast.69), channel_id=1, source_target_pairs={{0,3},{1,0},{2,1},{3,2},{4,7},{5,4},{6,5},{7,6},{8,11},{9,8},{10,9... | collective-permute-start | bytes 1376264 | tf_op jit(solution)/shard_map/ppermute | solution.py:58
  59.0 132.4 %collective-permute-start.7 = (bf16[512,4096]{1,0:T(8,128)(2,1)}, bf16[512,4096]{1,0:T(8,128)(2,1)}, u32[]{:S(2)}, u32[]{:S(2)}) collective-permute-start(bf16[512,4096]{1,0:T(8,128)(2,1)} %mine.1), channel_id=1, source_target_pairs={{0,16},{1,17},{2,18},{3,19},{4,20},{5,21},{6,22},{7,23},{8,24},{9,... | collective-permute-start | bytes 12582920 | tf_op jit(solution)/shard_map/ppermute | solution.py:58
  64.3 12.9 %copy-start.19 = (bf16[4,64,896]{2,1,0:T(8,128)(2,1)}, bf16[4,64,896]{2,1,0:T(8,128)(2,1)S(1)}, u32[]{:S(2)}) copy-start(bf16[4,64,896]{2,1,0:T(8,128)(2,1)S(1)} %collective-permute-done.13.refs_1_) | copy-start | bytes 1376260
  81.5 40.6 %collective-permute-start.16 = (bf16[1024,896]{1,0:T(8,128)(2,1)}, bf16[1024,896]{1,0:T(8,128)(2,1)S(1)}, u32[]{:S(2)}, u32[]{:S(2)}) collective-permute-start(bf16[1024,896]{1,0:T(8,128)(2,1)} %bitcast.59), channel_id=1, source_target_pairs={{0,64},{1,65},{2,66},{3,67},{4,68},{5,69},{6,70},{7,71},{8,72},{9,... | collective-permute-start | bytes 5505032 | tf_op jit(solution)/shard_map/ppermute | solution.py:58
  83.8 46.9 %collective-permute-start.17 = (bf16[1024,896]{1,0:T(8,128)(2,1)}, bf16[1024,896]{1,0:T(8,128)(2,1)}, u32[]{:S(2)}, u32[]{:S(2)}) collective-permute-start(bf16[1024,896]{1,0:T(8,128)(2,1)} %bitcast.60), channel_id=1, source_target_pairs={{0,192},{1,193},{2,194},{3,195},{4,196},{5,197},{6,198},{7,199},{8... | collective-permute-start | bytes 5505032 | tf_op jit(solution)/shard_map/ppermute | solution.py:58
  92.5 8.2 %collective-permute-start.26 = (bf16[256,896]{1,0:T(8,128)(2,1)}, bf16[256,896]{1,0:T(8,128)(2,1)S(1)}, u32[]{:S(2)}, u32[]{:S(2)}) collective-permute-start(bf16[256,896]{1,0:T(8,128)(2,1)} %get-tuple-element.28), channel_id=1, source_target_pairs={{0,1},{1,2},{2,3},{3,0},{4,5},{5,6},{6,7},{7,4},{8,9},{9,10},{10,1... | collective-permute-start | bytes 1376264 | tf_op jit(solution)/shard_map/ppermute | solution.py:58
  96.3 20.6 %collective-permute-start.21 = (bf16[512,896]{1,0:T(8,128)(2,1)}, bf16[512,896]{1,0:T(8,128)(2,1)S(1)}, u32[]{:S(2)}, u32[]{:S(2)}) collective-permute-start(bf16[512,896]{1,0:T(8,128)(2,1)} %shard_map.91), channel_id=1, source_target_pairs={{0,4},{1,5},{2,6},{3,7},{4,0},{5,1},{6,2},{7,3},{8,12},{9,13},{10,... | collective-permute-start | bytes 2752520 | tf_op jit(solution)/shard_map/ppermute | solution.py:58
  100.7 38.6 %collective-permute-start.19 = (bf16[512,1024]{1,0:T(8,128)(2,1)}, bf16[512,1024]{1,0:T(8,128)(2,1)S(1)}, u32[]{:S(2)}, u32[]{:S(2)}) collective-permute-start(bf16[512,1024]{1,0:T(8,128)(2,1)} %shard_map.89), channel_id=1, source_target_pairs={{0,4},{1,5},{2,6},{3,7},{4,0},{5,1},{6,2},{7,3},{8,12},{9,13},{10,... | collective-permute-start | bytes 3145736 | tf_op jit(solution)/shard_map/ppermute | solution.py:58
  116.9 33.3 %collective-permute-start.25 = (bf16[256,896]{1,0:T(8,128)(2,1)}, bf16[256,896]{1,0:T(8,128)(2,1)}, u32[]{:S(2)}, u32[]{:S(2)}) collective-permute-start(bf16[256,896]{1,0:T(8,128)(2,1)} %get-tuple-element.26), channel_id=1, source_target_pairs={{0,3},{1,0},{2,1},{3,2},{4,7},{5,4},{6,5},{7,6},{8,11},{9,8},{10,9... | collective-permute-start | bytes 1376264 | tf_op jit(solution)/shard_map/ppermute | solution.py:58
  122.2 8.5 %copy-start.1 = (bf16[1024,896]{1,0:T(8,128)(2,1)}, bf16[1024,896]{1,0:T(8,128)(2,1)S(1)}, u32[]{:S(2)}) copy-start(bf16[1024,896]{1,0:T(8,128)(2,1)S(1)} %collective-permute-done.16.refs_0_) | copy-start | bytes 5505028
  122.2 31.4 %collective-permute-start.27 = (bf16[256,896]{1,0:T(8,128)(2,1)S(1)}, bf16[256,896]{1,0:T(8,128)(2,1)}, u32[]{:S(2)}, u32[]{:S(2)}) collective-permute-start(bf16[256,896]{1,0:T(8,128)(2,1)S(1)} %add_convert_fusion.5), channel_id=1, source_target_pairs={{0,1},{1,2},{2,3},{3,0},{4,5},{5,6},{6,7},{7,4},{8,9},{9,10},{10,1... | collective-permute-start | bytes 1376264 | tf_op jit(solution)/shard_map/ppermute | solution.py:58
  140.3 9.9 %copy-start.2 = (bf16[1024,896]{1,0:T(8,128)(2,1)S(1)}, bf16[1024,896]{1,0:T(8,128)(2,1)}, u32[]{:S(2)}) copy-start(bf16[1024,896]{1,0:T(8,128)(2,1)} %shard_map.88.refs_9_.refs_1_) | copy-start | bytes 5505028
  140.3 13.3 %copy-start.7 = (f32[256,896]{1,0:T(8,128)S(1)}, f32[256,896]{1,0:T(8,128)}, u32[]{:S(2)}) copy-start(f32[256,896]{1,0:T(8,128)} %get-tuple-element.18.refs_8_) | copy-start | bytes 2752516
  150.1 28.6 %collective-permute-start.24 = (bf16[256,1792]{1,0:T(8,128)(2,1)}, bf16[256,1792]{1,0:T(8,128)(2,1)}, u32[]{:S(2)}, u32[]{:S(2)}) collective-permute-start(bf16[256,1792]{1,0:T(8,128)(2,1)} %get-tuple-element.25), channel_id=1, source_target_pairs={{0,1},{1,2},{2,3},{3,0},{4,5},{5,6},{6,7},{7,4},{8,9},{9,10},{10,1... | collective-permute-start | bytes 2752520 | tf_op jit(solution)/shard_map/ppermute | solution.py:58
  150.1 22.1 %copy-start.15 = (f32[256,896]{1,0:T(8,128)S(1)}, f32[256,896]{1,0:T(8,128)}, u32[]{:S(2)}) copy-start(f32[256,896]{1,0:T(8,128)} %get-tuple-element.30) | copy-start | bytes 2752516
  150.1 29.8 %copy-start.11 = (f32[256,1792]{1,0:T(8,128)S(1)}, f32[256,1792]{1,0:T(8,128)}, u32[]{:S(2)}) copy-start(f32[256,1792]{1,0:T(8,128)} %get-tuple-element.24) | copy-start | bytes 5505028
  150.1 17.6 %collective-permute-start.31 = (bf16[256,896]{1,0:T(8,128)(2,1)}, bf16[256,896]{1,0:T(8,128)(2,1)S(1)}, u32[]{:S(2)}, u32[]{:S(2)}) collective-permute-start(bf16[256,896]{1,0:T(8,128)(2,1)} %get-tuple-element.31), channel_id=1, source_target_pairs={{0,1},{1,2},{2,3},{3,0},{4,5},{5,6},{6,7},{7,4},{8,9},{9,10},{10,1... | collective-permute-start | bytes 1376264 | tf_op jit(solution)/shard_map/ppermute | solution.py:58
  150.2 41.2 %collective-permute-start.18 = (bf16[1024,896]{1,0:T(8,128)(2,1)S(1)}, bf16[1024,896]{1,0:T(8,128)(2,1)S(1)}, u32[]{:S(2)}, u32[]{:S(2)}) collective-permute-start(bf16[1024,896]{1,0:T(8,128)(2,1)S(1)} %copy-done.2), channel_id=1, source_target_pairs={{0,64},{1,65},{2,66},{3,67},{4,68},{5,69},{6,70},{7,71},{8,72},{9,... | collective-permute-start | bytes 5505032 | tf_op jit(solution)/shard_map/ppermute | solution.py:58
  154.9 22.4 %collective-permute-start.28 = (bf16[256,896]{1,0:T(8,128)(2,1)S(1)}, bf16[256,896]{1,0:T(8,128)(2,1)S(1)}, u32[]{:S(2)}, u32[]{:S(2)}) collective-permute-start(bf16[256,896]{1,0:T(8,128)(2,1)S(1)} %add_convert_fusion.4), channel_id=1, source_target_pairs={{0,8},{1,9},{2,10},{3,11},{4,12},{5,13},{6,14},{7,15},{8,0},{9,1},... | collective-permute-start | bytes 1376264 | tf_op jit(solution)/shard_map/ppermute | solution.py:58
  167.7 14.5 %collective-permute-start.6 = (f32[16,896]{1,0:T(8,128)S(1)}, f32[16,896]{1,0:T(8,128)S(1)}, u32[]{:S(2)}, u32[]{:S(2)}) collective-permute-start(f32[16,896]{1,0:T(8,128)S(1)} %dynamic-slice_bitcast_fusion), channel_id=1, source_target_pairs={{0,16},{1,17},{2,18},{3,19},{4,20},{5,21},{6,22},{7,23},{8,24},{9,... | collective-permute-start | bytes 172040 | tf_op jit(solution)/shard_map/ppermute | solution.py:58
  177.3 12.6 %collective-permute-start.30 = (bf16[256,896]{1,0:T(8,128)(2,1)}, bf16[256,896]{1,0:T(8,128)(2,1)S(1)}, u32[]{:S(2)}, u32[]{:S(2)}) collective-permute-start(bf16[256,896]{1,0:T(8,128)(2,1)} %get-tuple-element.29), channel_id=1, source_target_pairs={{0,3},{1,0},{2,1},{3,2},{4,7},{5,4},{6,5},{7,6},{8,11},{9,8},{10,9... | collective-permute-start | bytes 1376264 | tf_op jit(solution)/shard_map/ppermute | solution.py:58
  178.7 12.5 %collective-permute-start.32 = (bf16[256,896]{1,0:T(8,128)(2,1)S(1)}, bf16[256,896]{1,0:T(8,128)(2,1)S(1)}, u32[]{:S(2)}, u32[]{:S(2)}) collective-permute-start(bf16[256,896]{1,0:T(8,128)(2,1)S(1)} %add_convert_fusion.3), channel_id=1, source_target_pairs={{0,1},{1,2},{2,3},{3,0},{4,5},{5,6},{6,7},{7,4},{8,9},{9,10},{10,1... | collective-permute-start | bytes 1376264 | tf_op jit(solution)/shard_map/ppermute | solution.py:58
  182.2 9.0 %copy-start.8 = (f32[256,896]{1,0:T(8,128)S(1)}, f32[256,896]{1,0:T(8,128)}, u32[]{:S(2)}) copy-start(f32[256,896]{1,0:T(8,128)} %get-tuple-element.19.refs_8_) | copy-start | bytes 2752516
  182.2 29.8 %collective-permute-start.23 = (bf16[256,1792]{1,0:T(8,128)(2,1)}, bf16[256,1792]{1,0:T(8,128)(2,1)S(1)}, u32[]{:S(2)}, u32[]{:S(2)}) collective-permute-start(bf16[256,1792]{1,0:T(8,128)(2,1)} %get-tuple-element.23), channel_id=1, source_target_pairs={{0,3},{1,0},{2,1},{3,2},{4,7},{5,4},{6,5},{7,6},{8,11},{9,8},{10,9... | collective-permute-start | bytes 2752520 | tf_op jit(solution)/shard_map/ppermute | solution.py:58
  189.8 22.2 %collective-permute-start.29 = (bf16[256,1792]{1,0:T(8,128)(2,1)}, bf16[256,1792]{1,0:T(8,128)(2,1)}, u32[]{:S(2)}, u32[]{:S(2)}) collective-permute-start(bf16[256,1792]{1,0:T(8,128)(2,1)} %shard_map.96), channel_id=1, source_target_pairs={{0,1},{1,2},{2,3},{3,0},{4,5},{5,6},{6,7},{7,4},{8,9},{9,10},{10,1... | collective-permute-start | bytes 2752520 | tf_op jit(solution)/shard_map/ppermute | solution.py:58
  191.3 20.7 %collective-permute-start.33 = (bf16[256,896]{1,0:T(8,128)(2,1)S(1)}, bf16[256,896]{1,0:T(8,128)(2,1)S(1)}, u32[]{:S(2)}, u32[]{:S(2)}) collective-permute-start(bf16[256,896]{1,0:T(8,128)(2,1)S(1)} %add_convert_fusion.2), channel_id=1, source_target_pairs={{0,8},{1,9},{2,10},{3,11},{4,12},{5,13},{6,14},{7,15},{8,0},{9,1},... | collective-permute-start | bytes 1376264 | tf_op jit(solution)/shard_map/ppermute | solution.py:58
  192.7 18.6 %copy-start.24 = (f32[16,1792]{1,0:T(8,128)S(1)}, f32[16,1792]{1,0:T(8,128)}, u32[]{:S(2)}) copy-start(f32[16,1792]{1,0:T(8,128)} %param.9) | copy-start | bytes 344068
  192.7 18.6 %copy-start.25 = (f32[16,896]{1,0:T(8,128)S(1)}, f32[16,896]{1,0:T(8,128)}, u32[]{:S(2)}) copy-start(f32[16,896]{1,0:T(8,128)} %get-tuple-element.43) | copy-start | bytes 172036
  192.7 18.6 %copy-start.26 = (f32[16,896]{1,0:T(8,128)S(1)}, f32[16,896]{1,0:T(8,128)}, u32[]{:S(2)}) copy-start(f32[16,896]{1,0:T(8,128)} %get-tuple-element.44) | copy-start | bytes 172036
  192.7 19.3 %copy-start.3 = (f32[256,1792]{1,0:T(8,128)S(1)}, f32[256,1792]{1,0:T(8,128)}, u32[]{:S(2)}) copy-start(f32[256,1792]{1,0:T(8,128)} %get-tuple-element.20.refs_4_) | copy-start | bytes 5505028
  192.7 19.3 %copy-start.13 = (bf16[256,896]{1,0:T(8,128)(2,1)S(1)}, bf16[256,896]{1,0:T(8,128)(2,1)}, u32[]{:S(2)}) copy-start(bf16[256,896]{1,0:T(8,128)(2,1)} %copy-done.12) | copy-start | bytes 1376260
  209.1 5.6 %collective-permute-start.22 = (bf16[512,896]{1,0:T(8,128)(2,1)}, bf16[512,896]{1,0:T(8,128)(2,1)S(1)}, u32[]{:S(2)}, u32[]{:S(2)}) collective-permute-start(bf16[512,896]{1,0:T(8,128)(2,1)} %get-tuple-element.22), channel_id=1, source_target_pairs={{0,16},{1,17},{2,18},{3,19},{4,20},{5,21},{6,22},{7,23},{8,24},{9,... | collective-permute-start | bytes 2752520 | tf_op jit(solution)/shard_map/ppermute | solution.py:58
  (16 other events, 44.2 us)
